TPU v7x, 512 devices: a whole 4x8x8 slice. The times are simulated.
512 devices in a mesh: seq: 64 (over z, y_lo, x), head: 8 (over y_hi, core).
Axes of the slice: x: 4, y: 8 (y_hi: 4, y_lo: 2; y = y_hi * 2 + y_lo), z: 8, core: 2. Of those that a mesh axis runs over, the one named last changes fastest.
Arguments:
- queries: bfloat16 [65536, 4096], P(('seq', 'head')), may hold values from -5 to 5
- key_rows: bfloat16 [65536, 4096], P(('seq', 'head')), may hold values from -5 to 5
- value_rows: bfloat16 [65536, 4096], P(('seq', 'head')), may hold values from -6 to 6
- step_rates: bfloat16 [65536, 8], P(('seq', 'head')), may hold values from 0.1 to 9
- w_gate: bfloat16 [512, 8, 512], P('seq', 'head'), may hold values from -0.25 to 0.25
- w_up: bfloat16 [512, 8, 512], P('seq', 'head'), may hold values from -0.25 to 0.25
- w_down: bfloat16 [512, 8, 512], P('seq', 'head'), may hold values from -0.25 to 0.25
Outputs:
- block_out: bfloat16 [65536, 4096], P(('seq', 'head'))
All inputs are finite; a program needn't handle non-finite values.
Results may differ from a plain program's by a relative error of at most 0.012.
Values may be sent and summed in bfloat16 or wider, within the bound.
A program may use at most 64 MiB of HBM per device.

v0:
```python
import math

import jax
import jax.numpy as jnp
from jax import lax
from jax.sharding import Mesh
from jax.sharding import PartitionSpec as P

ATT_HEADS = 32
HEAD_DIM = 128
HEADS = 8
HS = 512
WINDOW = 64
SEQ_HEAD = ("seq_0", "seq_1", "seq_2", "head")
SEQ = ("seq_0", "seq_1", "seq_2")


STEP_SIZE = 0.05
NORM_EPS = 1e-06


def from_behind(value, axis, by):
    count = lax.axis_size(axis)
    pairs = [(i, i + by) for i in range(count) if 0 <= i + by < count]
    return lax.ppermute(value, axis, pairs)


def laid_out(tiles, dim):
    tiles = jnp.moveaxis(tiles, 0, dim)
    shape = tiles.shape
    return tiles.reshape(*shape[:dim], shape[dim] * shape[dim + 1], *shape[dim + 2 :])


def copy_for_each(value, axis):
    count = lax.axis_size(axis)
    return lax.all_to_all(
        jnp.broadcast_to(value[None], (count, *value.shape)), axis, 0, 0, tiled=True
    )


def gathered_copies(value, axis, dim):
    return laid_out(copy_for_each(value, axis), dim)


def cut_along(value, dim, count):
    before, after = (value.shape[:dim], value.shape[dim + 1 :])
    return jnp.moveaxis(value.reshape(*before, count, -1, *after), dim, 0)


def sum_at_owner(value, axis, dim):
    count = lax.axis_size(axis)
    tiles = lax.all_to_all(cut_along(value, dim, count), axis, 0, 0, tiled=True)
    return jnp.sum(tiles, axis=0)


def summed_rows(value, axes, dim):
    far, near = axes
    own = sum_at_owner(cut_along(value, dim, lax.axis_size(far)), near, dim + 1)
    return jnp.sum(lax.all_to_all(own, far, 0, 0, tiled=True), axis=0)


def rows_for(lines, count):
    spare = -lines.shape[0] % count
    if not spare:
        return lines
    return jnp.concatenate([lines, jnp.zeros((spare, *lines.shape[1:]), lines.dtype)])


def gathered_by_axis(value, axes, dim):
    far, near = axes
    leading = copy_for_each(value, far)
    tiles = jnp.swapaxes(copy_for_each(leading, near), 0, 1)
    return laid_out(tiles.reshape(-1, *value.shape), dim)


def total_of(value, axes):
    lines = value.reshape(-1, value.shape[-1])
    own = summed_rows(rows_for(lines, lax.axis_size(axes[0]) * lax.axis_size(axes[1])), axes, 0)
    whole = gathered_by_axis(own, axes, 0)
    return whole[: len(lines)].reshape(value.shape)


def local_attention(block_queries, key_span, value_span, start_pos):
    row_count = block_queries.shape[0]
    span_count = key_span.shape[0]
    query_heads = block_queries.reshape(row_count, ATT_HEADS, HEAD_DIM)
    key_heads = key_span.reshape(span_count, ATT_HEADS, HEAD_DIM)
    value_heads = value_span.reshape(span_count, ATT_HEADS, HEAD_DIM)
    scores = jnp.einsum(
        "qhd,khd->hqk", query_heads, key_heads, preferred_element_type=jnp.float32
    ) * (1.0 / math.sqrt(HEAD_DIM))
    query_pos = start_pos + lax.iota(jnp.int32, row_count)
    key_pos = start_pos - WINDOW + lax.iota(jnp.int32, span_count)
    allowed = (
        (key_pos[None, :] >= 0)
        & (key_pos[None, :] <= query_pos[:, None])
        & (key_pos[None, :] > query_pos[:, None] - WINDOW)
    )
    masked = jnp.where(allowed[None], scores, -1e30)
    maximum = jnp.max(masked, axis=2, keepdims=True)
    exp_scores = jnp.where(allowed[None], jnp.exp(masked - maximum), 0.0)
    totals = jnp.sum(exp_scores, axis=2)
    weights = exp_scores.astype(jnp.bfloat16)
    mixed = jnp.einsum("hqk,khd->qhd", weights, value_heads, preferred_element_type=jnp.float32)
    return (mixed / jnp.transpose(totals)[:, :, None]).reshape(row_count, ATT_HEADS * HEAD_DIM)


def rms_heads(tensor):
    blocks = tensor.astype(jnp.float32).reshape(tensor.shape[0], HEADS, HS)
    normed = blocks * lax.rsqrt(jnp.mean(blocks * blocks, axis=2, keepdims=True) + NORM_EPS)
    return normed.astype(jnp.bfloat16).reshape(tensor.shape[0], HEADS * HS)


def weight_columns(matrix, head, which):
    first = (3 * head + which) * HS
    return matrix[:, first : first + HS]


def renorm(old_rows, grad_rows, norm_scale):
    pieces = []
    for which in range(3):
        previous = weight_columns(old_rows, 0, which).astype(jnp.float32)
        stepped = previous - STEP_SIZE * norm_scale[0] * weight_columns(grad_rows, 0, which)
        factor = jnp.sqrt(jnp.mean(previous * previous, axis=-1, keepdims=True)) * lax.rsqrt(
            jnp.mean(stepped * stepped, axis=-1, keepdims=True) + NORM_EPS
        )
        pieces.append((stepped * factor).astype(jnp.bfloat16))
    return jnp.concatenate(pieces, 1)


def head_squares(grad_rows):
    sums = [jnp.sum(grad_rows * grad_rows)]
    return jnp.stack(sums)


def shards(queries, key_rows, value_rows, step_rates, w_gate, w_up, w_down):
    row_count = queries.shape[0]
    local_heads = w_gate.shape[1]
    start_pos = lax.axis_index(SEQ_HEAD) * row_count
    tail_rows = jnp.stack([key_rows[row_count - WINDOW :], value_rows[row_count - WINDOW :]])
    before = from_behind(tail_rows, SEQ_HEAD, 1)
    own_old = jnp.concatenate([w_gate, w_up, w_down], 2).reshape(
        w_gate.shape[0], local_heads * 3 * HS
    )
    stacked_old = gathered_copies(own_old, SEQ, 0)
    query_norm = rms_heads(queries)
    key_norm = rms_heads(key_rows)
    head_query, head_key, head_value, head_rate = (
        lax.all_to_all(query_norm, "head", split_axis=1, concat_axis=0, tiled=True),
        lax.all_to_all(key_norm, "head", split_axis=1, concat_axis=0, tiled=True),
        lax.all_to_all(value_rows, "head", split_axis=1, concat_axis=0, tiled=True),
        lax.all_to_all(step_rates, "head", split_axis=1, concat_axis=0, tiled=True),
    )
    attended = local_attention(
        queries,
        jnp.concatenate([before[0], key_rows], 0),
        jnp.concatenate([before[1], value_rows], 0),
        start_pos,
    )
    forward = []
    head = 0
    key_head = head_key
    gate_pre = jnp.dot(
        key_head, weight_columns(stacked_old, head, 0), preferred_element_type=jnp.float32
    )
    up_pre = jnp.dot(
        key_head, weight_columns(stacked_old, head, 1), preferred_element_type=jnp.float32
    )
    sigma_gate = jax.nn.sigmoid(gate_pre)
    silu_gate = gate_pre * sigma_gate
    hidden = (silu_gate * up_pre).astype(jnp.bfloat16)
    target = (
        -head_rate[:, head].astype(jnp.float32)[:, None] * head_value.astype(jnp.float32)
    ).astype(jnp.bfloat16)
    hidden_grad = jnp.einsum(
        "to,mo->tm",
        target,
        weight_columns(stacked_old, head, 2),
        preferred_element_type=jnp.float32,
    )
    gate_grad = (hidden_grad * up_pre * sigma_gate * (1.0 + gate_pre * (1.0 - sigma_gate))).astype(
        jnp.bfloat16
    )
    up_grad = (hidden_grad * silu_gate).astype(jnp.bfloat16)
    forward.append((key_head, hidden, target, gate_grad, up_grad))

    def grad_rows(start_row, count_rows):
        pieces = []
        key_head, hidden, target, gate_grad, up_grad = forward[0]
        pieces.append(
            jnp.einsum("ti,tm->im", key_head, gate_grad, preferred_element_type=jnp.float32)
        )
        pieces.append(
            jnp.einsum("ti,tm->im", key_head, up_grad, preferred_element_type=jnp.float32)
        )
        pieces.append(jnp.einsum("tm,to->mo", hidden, target, preferred_element_type=jnp.float32))
        return jnp.concatenate(pieces, 1)

    summed = total_of(grad_rows(0, HS), (("seq_0", "seq_1"), "seq_2"))
    norm_scale = lax.rsqrt(head_squares(summed) / (3 * HS * HS) + NORM_EPS)
    updated = renorm(stacked_old, summed, norm_scale)
    head = 0
    query_gate = jnp.dot(
        head_query, weight_columns(updated, head, 0), preferred_element_type=jnp.float32
    )
    query_up = jnp.dot(
        head_query, weight_columns(updated, head, 1), preferred_element_type=jnp.float32
    )
    query_hidden = (query_gate * jax.nn.sigmoid(query_gate) * query_up).astype(jnp.bfloat16)
    outputs = jnp.dot(
        query_hidden, weight_columns(updated, head, 2), preferred_element_type=jnp.float32
    ).astype(jnp.bfloat16)
    returned = lax.all_to_all(outputs, "head", split_axis=0, concat_axis=1, tiled=True)
    return (attended + returned.astype(jnp.float32)).astype(jnp.bfloat16)


def solution(mesh):
    torus = Mesh(
        mesh.devices.reshape(8, 2, 4, mesh.shape["head"]), ("seq_0", "seq_1", "seq_2", "head")
    )
    return jax.shard_map(
        shards,
        mesh=torus,
        in_specs=(
            P(SEQ_HEAD, None),
            P(SEQ_HEAD, None),
            P(SEQ_HEAD, None),
            P(SEQ_HEAD, None),
            P(SEQ, "head", None),
            P(SEQ, "head", None),
            P(SEQ, "head", None),
        ),
        out_specs=P(SEQ_HEAD, None),
        check_vma=False,
    )
```

profile of v0, /device:TPU:64, one launch (start us, length us, event | category | flops | bytes accessed | tf_op | source)
XLA Modules:
  0.0 372.0 jit_solution(16784414195117378475)
XLA Ops:
  1.3 7.1 %all-to-all-start.3 = ((bf16[128,8,1]{0,2,1:T(2,128)(2,1)}), bf16[128,8,1]{0,2,1:T(2,128)(2,1)S(1)}, u32[]{:S(2)}, u32[]{:S(2)}) async-start(bf16[128,8,1]{0,2,1:T(2,128)(2,1)} %copy.84), calls=%async_computation.3 | async-start | bytes 8192 | tf_op jit(solution)/shard_map/all_to_all | solution.py:152
  11.4 4.5 %all-to-all-done.3 = bf16[128,8,1]{0,2,1:T(2,128)(2,1)S(1)} async-done(((bf16[128,8,1]{0,2,1:T(2,128)(2,1)}), bf16[128,8,1]{0,2,1:T(2,128)(2,1)S(1)}, u32[]{:S(2)}, u32[]{:S(2)}) %all-to-all-start.3) | async-done | bytes 2080 | tf_op jit(solution)/shard_map/all_to_all | solution.py:152
  16.0 3.6 all-to-all-start.2
  19.6 2.3 copy.73
  21.9 26.6 %all-to-all-done.2 = bf16[128,8,512]{0,2,1:T(8,128)(2,1)S(1)} async-done(((bf16[128,8,512]{0,2,1:T(8,128)(2,1)}), bf16[128,8,512]{0,2,1:T(8,128)(2,1)S(1)}, u32[]{:S(2)}, u32[]{:S(2)}) %all-to-all-start.2) | async-done | bytes 1048608 | tf_op jit(solution)/shard_map/all_to_all | solution.py:150
  48.4 3.6 all-to-all-start.4
  52.1 29.3 %all-to-all-done.4 = bf16[128,8,512]{0,2,1:T(8,128)(2,1)S(1)} async-done(((bf16[128,8,512]{0,2,1:T(8,128)(2,1)}), bf16[128,8,512]{0,2,1:T(8,128)(2,1)S(1)}, u32[]{:S(2)}, u32[]{:S(2)}) %all-to-all-start.4) | async-done | bytes 1048608 | tf_op jit(solution)/shard_map/all_to_all | solution.py:151
  82.9 13.3 %all-to-all-start.1 = ((bf16[64,8,1536]{2,1,0:T(8,128)(2,1)}), bf16[64,8,1536]{2,1,0:T(8,128)(2,1)S(1)}, u32[]{:S(2)}, u32[]{:S(2)}) async-start(bf16[64,8,1536]{2,1,0:T(8,128)(2,1)} %broadcast_in_dim.30), calls=%async_computation.1 | async-start | bytes 3145728 | tf_op jit(solution)/shard_map/all_to_all | solution.py:36
  97.7 2.7 convert_bitcast_fusion.1
  100.4 2.9 copy.86
  103.3 2.8 fusion.5
  106.1 28.4 %all-to-all-done.1 = bf16[64,8,1536]{2,1,0:T(8,128)(2,1)S(1)} async-done(((bf16[64,8,1536]{2,1,0:T(8,128)(2,1)}), bf16[64,8,1536]{2,1,0:T(8,128)(2,1)S(1)}, u32[]{:S(2)}, u32[]{:S(2)}) %all-to-all-start.1) | async-done | bytes 1572896 | tf_op jit(solution)/shard_map/all_to_all | solution.py:36
  140.4 2.4 copy.87
  142.8 2.1 copy.88
  144.9 41.7 %all_to_all.102 = f32[4,16,8,1536]{3,2,1,0:T(8,128)S(1)} all-to-all(f32[4,16,8,1536]{3,2,1,0:T(8,128)S(1)} %copy.88), channel_id=1, replica_groups=mesh['seq_0'=8,'seq_1'=2,'seq_2'=4,'head'=8] {'seq_2'}, dimensions={0} | all-to-all | bytes 6291456 | tf_op jit(solution)/shard_map/all_to_all | solution.py:52
  187.8 4.4 %all-to-all-start.6 = ((f32[16,8,1536]{2,1,0:T(8,128)}), f32[16,8,1536]{2,1,0:T(8,128)S(1)}, u32[]{:S(2)}, u32[]{:S(2)}) async-start(f32[16,8,1536]{2,1,0:T(8,128)} %reduce_sum.111), calls=%async_computation.6 | async-start | bytes 1572864 | tf_op jit(solution)/shard_map/all_to_all | solution.py:59
  194.3 16.3 %all-to-all-done.6 = f32[16,8,1536]{2,1,0:T(8,128)S(1)} async-done(((f32[16,8,1536]{2,1,0:T(8,128)}), f32[16,8,1536]{2,1,0:T(8,128)S(1)}, u32[]{:S(2)}, u32[]{:S(2)}) %all-to-all-start.6) | async-done | bytes 786464 | tf_op jit(solution)/shard_map/all_to_all | solution.py:59
  210.6 3.6 all-to-all-start
  214.2 29.2 %all-to-all-done = bf16[128,8,512]{0,2,1:T(8,128)(2,1)S(1)} async-done(((bf16[128,8,512]{0,2,1:T(8,128)(2,1)}), bf16[128,8,512]{0,2,1:T(8,128)(2,1)S(1)}, u32[]{:S(2)}, u32[]{:S(2)}) %all-to-all-start) | async-done | bytes 1048608 | tf_op jit(solution)/shard_map/all_to_all | solution.py:149
  243.5 26.6 %all_to_all.103 = f32[16,8,1536]{2,1,0:T(8,128)S(1)} all-to-all(f32[16,8,1536]{2,1,0:T(8,128)S(1)} %broadcast_in_dim.31), channel_id=1, replica_groups=mesh['seq_0'=8,'seq_1'=2,'seq_2'=4,'head'=8] {'seq_0','seq_1'}, dimensions={0} | all-to-all | bytes 1572864 | tf_op jit(solution)/shard_map/all_to_all | solution.py:36
  270.1 2.0 broadcast_in_dim.32
  272.2 3.7 all-to-all-start.8
  279.2 2.1 collective-permute-start
  281.3 2.3 copy.75
  283.6 2.3 copy.78
  285.9 2.3 copy.81
  288.1 37.1 %all-to-all-done.8 = f32[4,16,8,1536]{3,2,1,0:T(8,128)S(1)} async-done(((f32[4,16,8,1536]{3,2,1,0:T(8,128)}), f32[4,16,8,1536]{3,2,1,0:T(8,128)S(1)}, u32[]{:S(2)}, u32[]{:S(2)}) %all-to-all-start.8) | async-done | bytes 3145760 | tf_op jit(solution)/shard_map/all_to_all | solution.py:36
  330.5 2.2 fusion.27
  332.6 4.8 %convolution_convert_fusion = bf16[1024,512]{1,0:T(8,128)(2,1)} fusion(f32[1024,512]{1,0:T(8,128)} %fusion.27, bf16[1024,512]{1,0:T(8,128)(2,1)S(1)} %bitcast.107, f32[512,1536]{1,0:T(8,128)} %bitcast.95, f32[512]{0:T(512)S(1)} %get-tuple-element.20, f32[512]{0:T(512)S(1)} %get-tuple-element.21, f32[]{:T(128)S(6)} %mul.208, bf16[512,1536]{1,0:T(8,128)(2,1)S(1)} %bitcast.92), kind=kOutput, calls=%fused_computation.38 | convolution fusion | flops 1080033280 | bytes 7345152 | tf_op jit(solution)/shard_map/dot_general | solution.py:210
  337.4 3.6 all-to-all-start.9
  346.0 2.1 bitcast_divide_fusion
  350.1 20.2 %all-to-all-done.9 = bf16[8,128,512]{2,1,0:T(8,128)(2,1)S(1)} async-done(((bf16[8,128,512]{2,1,0:T(8,128)(2,1)}), bf16[8,128,512]{2,1,0:T(8,128)(2,1)S(1)}, u32[]{:S(2)}, u32[]{:S(2)}) %all-to-all-start.9) | async-done | bytes 1048608 | tf_op jit(solution)/shard_map/all_to_all | solution.py:213
  (81 shorter events, 33.1 us)
Async XLA Ops:
  1.3 14.7 %all-to-all-start.3 = ((bf16[128,8,1]{0,2,1:T(2,128)(2,1)}), bf16[128,8,1]{0,2,1:T(2,128)(2,1)S(1)}, u32[]{:S(2)}, u32[]{:S(2)}) async-start(bf16[128,8,1]{0,2,1:T(2,128)(2,1)} %copy.84), calls=%async_computation.3 | async-start | bytes 8192 | tf_op jit(solution)/shard_map/all_to_all | solution.py:152
  10.0 6.0 %copy-start.4 = (bf16[128,4096]{0,1:T(8,128)(2,1)}, bf16[128,4096]{0,1:T(8,128)(2,1)S(1)}, u32[]{:S(2)}) copy-start(bf16[128,4096]{0,1:T(8,128)(2,1)S(1)} %copy.76) | copy-start | bytes 3145732
  16.0 32.5 %all-to-all-start.2 = ((bf16[128,8,512]{0,2,1:T(8,128)(2,1)}), bf16[128,8,512]{0,2,1:T(8,128)(2,1)S(1)}, u32[]{:S(2)}, u32[]{:S(2)}) async-start(bf16[128,8,512]{0,2,1:T(8,128)(2,1)} %bitcast.105), calls=%async_computation.2 | async-start | bytes 2097152 | tf_op jit(solution)/shard_map/all_to_all | solution.py:150
  19.6 32.5 %copy-start.14 = (bf16[8,1,512]{2,0,1:T(8,128)(2,1)S(1)}, bf16[8,1,512]{2,0,1:T(8,128)(2,1)}, u32[]{:S(2)}) copy-start(bf16[8,1,512]{2,0,1:T(8,128)(2,1)} %param.13) | copy-start | bytes 24580
  19.6 32.5 %copy-start.15 = (bf16[8,1,512]{2,0,1:T(8,128)(2,1)S(1)}, bf16[8,1,512]{2,0,1:T(8,128)(2,1)}, u32[]{:S(2)}) copy-start(bf16[8,1,512]{2,0,1:T(8,128)(2,1)} %param.12) | copy-start | bytes 24580
  19.6 32.5 %copy-start.16 = (bf16[8,1,512]{2,0,1:T(8,128)(2,1)S(1)}, bf16[8,1,512]{2,0,1:T(8,128)(2,1)}, u32[]{:S(2)}) copy-start(bf16[8,1,512]{2,0,1:T(8,128)(2,1)} %param.11) | copy-start | bytes 24580
  48.4 34.4 %copy-start.8 = (bf16[128,8,512]{0,2,1:T(8,128)(2,1)}, bf16[128,8,512]{0,2,1:T(8,128)(2,1)S(1)}, u32[]{:S(2)}) copy-start(bf16[128,8,512]{0,2,1:T(8,128)(2,1)S(1)} %all-to-all-done.2) | copy-start | bytes 3145732
  48.4 32.9 %all-to-all-start.4 = ((bf16[128,8,512]{0,2,1:T(8,128)(2,1)}), bf16[128,8,512]{0,2,1:T(8,128)(2,1)S(1)}, u32[]{:S(2)}, u32[]{:S(2)}) async-start(bf16[128,8,512]{0,2,1:T(8,128)(2,1)} %bitcast.23), calls=%async_computation.4 | async-start | bytes 2097152 | tf_op jit(solution)/shard_map/all_to_all | solution.py:151
  81.4 1.5 copy-start.5
  82.9 51.5 %all-to-all-start.1 = ((bf16[64,8,1536]{2,1,0:T(8,128)(2,1)}), bf16[64,8,1536]{2,1,0:T(8,128)(2,1)S(1)}, u32[]{:S(2)}, u32[]{:S(2)}) async-start(bf16[64,8,1536]{2,1,0:T(8,128)(2,1)} %broadcast_in_dim.30), calls=%async_computation.1 | async-start | bytes 3145728 | tf_op jit(solution)/shard_map/all_to_all | solution.py:36
  134.4 1.4 copy-start
  135.1 1.2 copy-start.6
  187.8 4.4 %copy-start.9 = (bf16[128,4096]{1,0:T(8,128)(2,1)S(1)}, bf16[128,4096]{1,0:T(8,128)(2,1)}, u32[]{:S(2)}) copy-start(bf16[128,4096]{1,0:T(8,128)(2,1)} %param.7) | copy-start | bytes 3145732
  187.8 22.8 %all-to-all-start.6 = ((f32[16,8,1536]{2,1,0:T(8,128)}), f32[16,8,1536]{2,1,0:T(8,128)S(1)}, u32[]{:S(2)}, u32[]{:S(2)}) async-start(f32[16,8,1536]{2,1,0:T(8,128)} %reduce_sum.111), calls=%async_computation.6 | async-start | bytes 1572864 | tf_op jit(solution)/shard_map/all_to_all | solution.py:59
  210.6 32.9 %all-to-all-start = ((bf16[128,8,512]{0,2,1:T(8,128)(2,1)}), bf16[128,8,512]{0,2,1:T(8,128)(2,1)S(1)}, u32[]{:S(2)}, u32[]{:S(2)}) async-start(bf16[128,8,512]{0,2,1:T(8,128)(2,1)} %bitcast.10), calls=%async_computation | async-start | bytes 2097152 | tf_op jit(solution)/shard_map/all_to_all | solution.py:149
  243.4 28.8 %copy-start.7 = (bf16[128,8,512]{0,2,1:T(8,128)(2,1)}, bf16[128,8,512]{0,2,1:T(8,128)(2,1)S(1)}, u32[]{:S(2)}) copy-start(bf16[128,8,512]{0,2,1:T(8,128)(2,1)S(1)} %all-to-all-done) | copy-start | bytes 3145732
  272.2 53.0 %all-to-all-start.8 = ((f32[4,16,8,1536]{3,2,1,0:T(8,128)}), f32[4,16,8,1536]{3,2,1,0:T(8,128)S(1)}, u32[]{:S(2)}, u32[]{:S(2)}) async-start(f32[4,16,8,1536]{3,2,1,0:T(8,128)} %broadcast_in_dim.32), calls=%async_computation.8 | async-start | bytes 6291456 | tf_op jit(solution)/shard_map/all_to_all | solution.py:36
  279.2 62.0 %collective-permute-start = (bf16[2,64,4096]{2,1,0:T(8,128)(2,1)}, bf16[2,64,4096]{2,1,0:T(8,128)(2,1)}, u32[]{:S(2)}, u32[]{:S(2)}) collective-permute-start(bf16[2,64,4096]{2,1,0:T(8,128)(2,1)} %pad_maximum_fusion.1), channel_id=1, source_target_pairs={{0,1},{1,2},{2,3},{3,4},{4,5},{5,6},{6,7},{7,8},{8,9},{9,10},{10,1... | collective-permute-start | bytes 3145736 | tf_op jit(solution)/shard_map/ppermute | solution.py:25
  327.2 2.0 copy-start.1
  327.5 2.7 copy-start.3
  329.2 1.2 copy-start.12
  330.5 2.2 copy-start.2
  337.4 32.8 %all-to-all-start.9 = ((bf16[8,128,512]{2,1,0:T(8,128)(2,1)}), bf16[8,128,512]{2,1,0:T(8,128)(2,1)S(1)}, u32[]{:S(2)}, u32[]{:S(2)}) async-start(bf16[8,128,512]{2,1,0:T(8,128)(2,1)} %bitcast.111), calls=%async_computation.9 | async-start | bytes 2097152 | tf_op jit(solution)/shard_map/all_to_all | solution.py:213
  342.4 1.2 copy-start.10
  342.4 1.5 copy-start.11
  344.8 1.2 copy-start.13
where the time goes:
time: 373 us; the launch traced here: 372 us
  waiting for transfers between devices  192 us (51%)
  blocking collectives  68.3 us (18%)
  starting transfers between devices  44.8 us (12%)
  local copies, waits for them, and re-layouts  35.1 us (9%)
  other arithmetic  16.1 us (4%)
  matrix products  15 us (4%)
    all_to_all x2, waiting for transfers between devices, copy_for_each(): lax.all_to_all(jnp.broadcast_to(value[None], (count, *value.shape)), axis...  65.4 us
    all_to_all x1, blocking collectives, sum_at_owner(): tiles = lax.all_to_all(cut_along(value, dim, count), axis, 0, 0, tiled=True)  41.7 us
    all_to_all x1, waiting for transfers between devices, shards(): lax.all_to_all(value_rows, 'head', split_axis=1, concat_axis=0, tiled=True)  29.3 us
    all_to_all x1, waiting for transfers between devices, shards(): lax.all_to_all(query_norm, 'head', split_axis=1, concat_axis=0, tiled=True)  29.2 us
    all_to_all x1, blocking collectives, copy_for_each(): lax.all_to_all(jnp.broadcast_to(value[None], (count, *value.shape)), axis...  26.6 us
    all_to_all x1, waiting for transfers between devices, shards(): lax.all_to_all(key_norm, 'head', split_axis=1, concat_axis=0, tiled=True)  26.6 us
    all_to_all x1, waiting for transfers between devices, shards(): lax.all_to_all(outputs, 'head', split_axis=0, concat_axis=1, tiled=True)  20.2 us
    all_to_all x2, starting transfers between devices, copy_for_each(): lax.all_to_all(jnp.broadcast_to(value[None], (count, *value.shape)), axis...  17 us
  transfers between devices with their start and end apart: 9, of which 8 were waited for; matrix products, arithmetic and copies ran while one was open for 12% of the time, Pallas kernels for 0%

commit v1 on v0

v1 whole, which is shorter than its diff:
```python
import math

import jax
import jax.numpy as jnp
from jax import lax
from jax.experimental import pallas as pl
from jax.experimental.pallas import tpu as pltpu
from jax.sharding import Mesh
from jax.sharding import PartitionSpec as P

HEAD_DIM = 128
HEADS = 8
HS = 512
WINDOW = 64
STEP_SIZE = 0.05
NORM_EPS = 1e-06
ROWS = 128
D = HEADS * HS
NX, NY, NZ = 4, 8, 8
AXES = ("z", "yl", "x", "yh", "c")
MESH = pl.DeviceIdType.MESH
F32, BF16 = jnp.float32, jnp.bfloat16
WAYS = ((1, 0, 1, 0), (7, 0, -1, 0), (3, 0, 0, 1), (5, 0, 0, -1), (2, 1, 0, 0), (6, -1, 0, 0), (4, 0, 1, 1))
OWN = len(WAYS)


def fast_kernel(
    q_hbm, k_hbm, v_hbm, rate_ref, w_ref, out_ref,
    ql, kl, vl, tl, halo, kb, vb, qb, wrecv, wfull, gu, hid, gown, gsend, gex, gb, rsb, agb, wnew, fo, ret, att,
    lsem, wsend, wrecv_sem, wfsend, wfrecv, ksend, krecv, vsend, vrecv, qsend, qrecv, hsend, hrecv,
    exsend, exrecv, rssend, rsrecv, agsend, agrecv, agfsend, agfrecv, osend, orecv,
):
    z, yl, x, yh, c = (lax.axis_index(a) for a in AXES)
    y = 2 * yh + yl
    colour = lax.rem(2 * x + y + 3 * z, 8)
    sign = 1 - 2 * c
    other = (z, yl, x, yh, 1 - c)
    spot = z * NX + x

    def device(px, py, pz, core):
        py = lax.rem(py + 64, NY)
        return (lax.rem(pz + 64, NZ), lax.rem(py, 2), lax.rem(px + 64, NX), py // 2, core)

    def there(way, back=1):
        _, dx, dy, dz = WAYS[way]
        turn = sign if way == OWN - 1 else 1
        return device(x + back * dx, y + back * turn * dy, z + back * turn * dz, c)

    def head_of(way):
        return colour if way == OWN else lax.rem(colour + WAYS[way][0], 8)

    def remote(src, dst, send, recv, dev):
        return pltpu.make_async_remote_copy(
            src_ref=src, dst_ref=dst, send_sem=send, recv_sem=recv, device_id=dev, device_id_type=MESH
        )

    def columns(head):
        return pl.ds(pl.multiple_of(head * HS, HS), HS)

    loads = [pltpu.make_async_copy(v_hbm, vl, lsem.at[0]), pltpu.make_async_copy(k_hbm, kl, lsem.at[1]),
             pltpu.make_async_copy(q_hbm, ql, lsem.at[2])]
    for load in loads:
        load.start()
    for way in range(OWN):
        remote(k_hbm.at[:, columns(head_of(way))], kb.at[way], ksend, krecv.at[way], there(way)).start()

    my_head = 2 * yh + c
    is_self = (my_head == colour) & (yl == c)

    def weight_dest(dx, dz):
        px, pz = x + dx, z + dz
        return device(px, my_head - 2 * px - 3 * pz, pz, yl)

    @pl.when(is_self)
    def _():
        wrecv[yl, spot] = w_ref[...]

    @pl.when(jnp.logical_not(is_self))
    def _():
        remote(w_ref, wrecv.at[yl, spot], wsend, wrecv_sem.at[0], weight_dest(0, 0)).start()

    def send_weights(i, carry):
        dx, dz = lax.rem(i, NX), i // NX
        remote(w_ref, wrecv.at[yl, spot], wsend, wrecv_sem.at[dz], weight_dest(dx, dz)).start()
        return carry

    lax.fori_loop(1, NX * NZ, send_weights, 0)

    loads[0].wait()
    for head in range(HEADS):
        rate = rate_ref[:, head : head + 1].astype(F32)
        tl[head] = (-rate * vl[:, head * HS : (head + 1) * HS].astype(F32)).astype(BF16)
    for way in range(OWN):
        remote(tl.at[head_of(way)], vb.at[way], vsend, vrecv.at[way], there(way)).start()
    vb[OWN] = tl[colour]
    loads[1].wait()
    kb[OWN] = kl[:, columns(colour)]

    def unpack(half, pz):
        for pair in range(NX // 2):
            one = wrecv[half, pz * NX + 2 * pair].astype(F32)
            two = wrecv[half, pz * NX + 2 * pair + 1].astype(F32)
            rows = pl.ds(pl.multiple_of(((pz * 2 + half) * NX + 2 * pair) * 8, 16), 16)
            wfull[rows, : 3 * HS // 2] = jnp.concatenate([one[:8], two[:8]], 0).astype(BF16)
            wfull[rows, 3 * HS // 2 :] = jnp.concatenate([one[8:], two[8:]], 0).astype(BF16)

    def weights_in(dz, carry):
        pz = lax.rem(z - dz + NZ, NZ)

        @pl.when(is_self & (dz == 0))
        def _():
            part = wrecv.at[c, pl.ds(0, NX - 1)]
            remote(part, part, wsend, wrecv_sem.at[dz], other).wait_recv()

        @pl.when(jnp.logical_not(is_self & (dz == 0)))
        def _():
            part = wrecv.at[c, pl.ds(0, NX)]
            remote(part, part, wsend, wrecv_sem.at[dz], other).wait_recv()

        part = wrecv.at[c, pl.ds(pz * NX, NX)]
        remote(part, part, wfsend, wfrecv, other).start()
        unpack(c, pz)
        return carry

    lax.fori_loop(0, NZ, weights_in, 0)

    def normed(block):
        wide = block.astype(F32)
        return (wide * lax.rsqrt(jnp.mean(wide * wide, axis=-1, keepdims=True) + NORM_EPS)).astype(BF16)

    for way in range(OWN + 1):
        if way < OWN:
            remote(kb.at[way], kb.at[way], ksend, krecv.at[way], other).wait_recv()
        kb[way] = normed(kb[way])

    remote(wrecv.at[1 - c], wrecv.at[1 - c], wfsend, wfrecv, other).wait_recv()

    def unpack_other(pz, carry):
        unpack(1 - c, pz)
        return carry

    lax.fori_loop(0, NZ, unpack_other, 0)

    for way in range(OWN):
        remote(vb.at[way], vb.at[way], vsend, vrecv.at[way], other).wait_recv()

    for way in range(OWN):
        remote(q_hbm.at[:, columns(head_of(way))], qb.at[way], qsend, qrecv.at[way], there(way)).start()
    place = (((z * 2 + yl) * NX + x) * 4 + yh) * 2 + c
    after = lax.rem(place + 1, 512)
    next_block = (after // 64, lax.rem(after // 32, 2), lax.rem(after // 8, 4), lax.rem(after // 2, 4), lax.rem(after, 2))
    remote(kl.at[pl.ds(ROWS - WINDOW, WINDOW)], halo.at[0], hsend, hrecv, next_block).start()
    remote(vl.at[pl.ds(ROWS - WINDOW, WINDOW)], halo.at[1], hsend, hrecv, next_block).start()
    loads[2].wait()
    qb[OWN] = normed(ql[:, columns(colour)])

    def tokens(i, carry):
        keys = kb[pl.ds(2 * i, 2)].reshape(2 * ROWS, HS)
        target = vb[pl.ds(2 * i, 2)].reshape(2 * ROWS, HS)
        gate_pre = jnp.dot(keys, wfull[:, :HS], preferred_element_type=F32)
        up_pre = jnp.dot(keys, wfull[:, HS : 2 * HS], preferred_element_type=F32)
        hidden_grad = lax.dot_general(
            target, wfull[:, 2 * HS :], (((1,), (1,)), ((), ())), preferred_element_type=F32
        )
        sigma = jax.nn.sigmoid(gate_pre)
        silu = gate_pre * sigma
        hid[pl.ds(2 * i, 2)] = (silu * up_pre).astype(BF16).reshape(2, ROWS, HS)
        gate_grad = (hidden_grad * up_pre * sigma * (1.0 + gate_pre * (1.0 - sigma))).astype(BF16)
        up_grad = (hidden_grad * silu).astype(BF16)
        for half in range(2):
            part = slice(half * HS // 2, (half + 1) * HS // 2)
            gu[half, pl.ds(2 * i, 2), :, : HS // 2] = gate_grad[:, part].reshape(2, ROWS, HS // 2)
            gu[half, pl.ds(2 * i, 2), :, HS // 2 :] = up_grad[:, part].reshape(2, ROWS, HS // 2)
        return carry

    lax.fori_loop(0, 4, tokens, 0)

    def half_sums(half, store):
        def rows(i, carry):
            span = pl.ds(pl.multiple_of(i * 256, 256), 256)
            keys = kb[:, :, span].reshape(8 * ROWS, 256)
            grads = gu[half].reshape(8 * ROWS, HS)
            hidden = hid[:, :, span].reshape(8 * ROWS, 256)
            target = vb[:, :, pl.ds(pl.multiple_of(half * 256, 256), 256)].reshape(8 * ROWS, 256)
            over_tokens = (((0,), (0,)), ((), ()))
            store[span, :HS] = lax.dot_general(keys, grads, over_tokens, preferred_element_type=F32).astype(store.dtype)
            store[span, HS:] = lax.dot_general(hidden, target, over_tokens, preferred_element_type=F32).astype(store.dtype)
            return carry

        lax.fori_loop(0, 2, rows, 0)

    half_sums(1 - c, gsend)
    exchange = remote(gsend, gex, exsend, exrecv, other)
    exchange.start()
    half_sums(c, gown)
    exchange.wait_recv()

    def mate(dx, dz):
        return device(x + dx, y - 2 * dx - 3 * dz, z + dz, c)

    def send_sums(dz, carry):
        pz = lax.rem(z + dz, NZ)
        rows = pl.ds(pl.multiple_of(pz * 64, 64), 64)
        gb[pl.ds(pz * NX, NX)] = (gown[rows, :] + gex[rows, :].astype(F32)).astype(BF16).reshape(NX, 16, 3 * HS // 2)
        for dx in range(NX):
            px = lax.rem(x + dx, NX)

            def go():
                remote(gb.at[pz * NX + px], rsb.at[spot], rssend, rsrecv, mate(dx, dz)).start()

            if dx == 0:
                pl.when(dz > 0)(go)
            else:
                go()
        return carry

    lax.fori_loop(0, NZ, send_sums, 0)
    rsb[spot] = gb[spot]

    remote(halo, halo, hsend, hrecv, other).wait_recv()
    span_rows = ROWS + WINDOW
    at_row = lax.broadcasted_iota(jnp.int32, (ROWS, span_rows), 0)
    at_key = lax.broadcasted_iota(jnp.int32, (ROWS, span_rows), 1)
    allowed = (at_key > at_row) & (at_key <= at_row + WINDOW) & (at_key + place * ROWS >= WINDOW)

    def attend(head, carry):
        cols = columns(head)
        queries = ql[:, cols]
        keys = jnp.concatenate([halo[0, :, cols], kl[:, cols]], 0)
        values = jnp.concatenate([halo[1, :, cols], vl[:, cols]], 0)
        for sub in range(HS // HEAD_DIM):
            part = slice(sub * HEAD_DIM, (sub + 1) * HEAD_DIM)
            scores = lax.dot_general(
                queries[:, part], keys[:, part], (((1,), (1,)), ((), ())), preferred_element_type=F32
            ) * (1.0 / math.sqrt(HEAD_DIM))
            masked = jnp.where(allowed, scores, -1e30)
            maximum = jnp.max(masked, axis=1, keepdims=True)
            weights = jnp.where(allowed, jnp.exp(masked - maximum), 0.0)
            totals = jnp.sum(weights, axis=1, keepdims=True)
            mixed = jnp.dot(weights.astype(BF16), values[:, part], preferred_element_type=F32)
            att[head, :, part] = mixed / totals
        return carry

    lax.fori_loop(0, HEADS, attend, 0)

    for way in range(OWN):
        remote(qb.at[way], qb.at[way], qsend, qrecv.at[way], other).wait_recv()
        qb[way] = normed(qb[way])

    others = rsb.at[pl.ds(0, NX * NZ - 1)]
    remote(others, others, rssend, rsrecv, other).wait_recv()

    def add_up(i, total):
        return total + jnp.sum(rsb[pl.ds(i * NX, NX)].astype(F32), axis=0)

    agb[c, spot] = lax.fori_loop(0, NZ, add_up, jnp.zeros((16, 3 * HS // 2), F32)).astype(BF16)

    def spread(i, carry):
        dx, dz = lax.rem(i, NX), i // NX
        remote(agb.at[c, spot], agb.at[c, spot], agsend, agrecv.at[dz], mate(dx, dz)).start()
        return carry

    lax.fori_loop(1, NX * NZ, spread, 0)

    def sums_in(dz, carry):
        pz = lax.rem(z - dz + NZ, NZ)

        @pl.when(dz == 0)
        def _():
            part = agb.at[c, pl.ds(0, NX - 1)]
            remote(part, part, agsend, agrecv.at[dz], other).wait_recv()

        @pl.when(dz > 0)
        def _():
            part = agb.at[c, pl.ds(0, NX)]
            remote(part, part, agsend, agrecv.at[dz], other).wait_recv()

        part = agb.at[c, pl.ds(pz * NX, NX)]
        remote(part, part, agfsend, agfrecv, other).start()
        return carry

    lax.fori_loop(0, NZ, sums_in, 0)
    remote(agb.at[1 - c], agb.at[1 - c], agfsend, agfrecv, other).wait_recv()

    def squares(i, total):
        for half in range(2):
            part = agb[half, pl.ds(i * NX, NX)].astype(F32).reshape(64, 3 * HS // 2)
            total = total + jnp.sum(part * part, axis=0, keepdims=True)
        return total

    square_sum = jnp.sum(lax.fori_loop(0, NZ, squares, jnp.zeros((1, 3 * HS // 2), F32)), axis=1, keepdims=True)
    step = STEP_SIZE * lax.rsqrt(square_sum * (1.0 / (3 * HS * HS)) + NORM_EPS)

    def renorm(i, carry):
        rows = pl.ds(pl.multiple_of(i * 64, 64), 64)
        low = agb[0, pl.ds(i * NX, NX)].astype(F32).reshape(64, 3 * HS // 2)
        high = agb[1, pl.ds(i * NX, NX)].astype(F32).reshape(64, 3 * HS // 2)
        for which in range(3):
            part = slice(which * HS // 2, (which + 1) * HS // 2)
            grads = jnp.concatenate([low[:, part], high[:, part]], 1)
            previous = wfull[rows, which * HS : (which + 1) * HS].astype(F32)
            stepped = previous - step * grads
            factor = jnp.sqrt(jnp.mean(previous * previous, axis=-1, keepdims=True)) * lax.rsqrt(
                jnp.mean(stepped * stepped, axis=-1, keepdims=True) + NORM_EPS
            )
            wnew[rows, which * HS : (which + 1) * HS] = (stepped * factor).astype(BF16)
        return carry

    lax.fori_loop(0, NZ, renorm, 0)

    for pair in range(4):
        queries = qb[2 * pair : 2 * pair + 2].reshape(2 * ROWS, HS)
        gate = jnp.dot(queries, wnew[:, :HS], preferred_element_type=F32)
        up = jnp.dot(queries, wnew[:, HS : 2 * HS], preferred_element_type=F32)
        hidden = (gate * jax.nn.sigmoid(gate) * up).astype(BF16)
        result = jnp.dot(hidden, wnew[:, 2 * HS :], preferred_element_type=F32)
        fo[2 * pair : 2 * pair + 2] = result.astype(BF16).reshape(2, ROWS, HS)
        for way in (2 * pair, 2 * pair + 1):
            if way < OWN:
                remote(fo.at[way], ret.at[way], osend, orecv.at[way], there(way, -1)).start()
    ret[OWN] = fo[OWN]
    for way in (OWN, *range(OWN)):
        if way < OWN:
            remote(ret.at[way], ret.at[way], osend, orecv.at[way], other).wait_recv()
        head = head_of(way)
        out_ref[:, columns(head)] = (att[head] + ret[way].astype(F32)).astype(BF16)

    for buffer, sem in ((kb, ksend), (vb, vsend), (qb, qsend), (ret, osend)):
        sent = buffer.at[pl.ds(0, OWN)]
        remote(sent, sent, sem, orecv.at[0], other).wait_send()
    remote(halo, halo, hsend, hrecv, other).wait_send()
    exchange.wait_send()
    for buffer, sem in ((rsb, rssend), (agb.at[0], agsend)):
        sent = buffer.at[pl.ds(0, NX * NZ - 1)]
        remote(sent, sent, sem, orecv.at[0], other).wait_send()

    @pl.when(is_self)
    def _():
        sent = wrecv.at[0, pl.ds(0, NX * NZ - 1)]
        remote(sent, sent, wsend, orecv.at[0], other).wait_send()

    @pl.when(jnp.logical_not(is_self))
    def _():
        remote(wrecv.at[0], wrecv.at[0], wsend, orecv.at[0], other).wait_send()

    for buffer, sem in ((wrecv.at[0], wfsend), (agb.at[0], agfsend)):
        remote(buffer, buffer, sem, orecv.at[0], other).wait_send()


def shards(queries, key_rows, value_rows, step_rates, w_gate, w_up, w_down):
    own = jnp.concatenate([w_gate, w_up, w_down], 2).reshape(8, 3 * HS)
    own = jnp.concatenate([own[:, : 3 * HS // 2], own[:, 3 * HS // 2 :]], 0)
    hbm = pl.BlockSpec(memory_space=pl.ANY)
    vmem = pl.BlockSpec(memory_space=pltpu.VMEM)
    wide = 3 * HS // 2
    blocks = pltpu.VMEM((8, ROWS, HS), BF16)
    dma = pltpu.SemaphoreType.DMA
    return pl.pallas_call(
        fast_kernel,
        out_shape=jax.ShapeDtypeStruct((ROWS, D), BF16),
        in_specs=[hbm, hbm, hbm, vmem, vmem],
        out_specs=vmem,
        scratch_shapes=[
            pltpu.VMEM((ROWS, D), BF16),
            pltpu.VMEM((ROWS, D), BF16),
            pltpu.VMEM((ROWS, D), BF16),
            blocks,
            pltpu.VMEM((2, WINDOW, D), BF16),
            blocks,
            blocks,
            blocks,
            pltpu.VMEM((2, NZ * NX, 16, wide), BF16),
            pltpu.VMEM((HS, 3 * HS), BF16),
            pltpu.VMEM((2, 8, ROWS, HS), BF16),
            blocks,
            pltpu.VMEM((HS, wide), F32),
            pltpu.VMEM((HS, wide), BF16),
            pltpu.VMEM((HS, wide), BF16),
            pltpu.VMEM((NZ * NX, 16, wide), BF16),
            pltpu.VMEM((NZ * NX, 16, wide), BF16),
            pltpu.VMEM((2, NZ * NX, 16, wide), BF16),
            pltpu.VMEM((HS, 3 * HS), BF16),
            blocks,
            blocks,
            pltpu.VMEM((8, ROWS, HS), F32),
            dma((3,)),
            dma, dma((NZ,)), dma, dma,
            dma, dma((OWN,)), dma, dma((OWN,)), dma, dma((OWN,)),
            dma, dma,
            dma, dma,
            dma, dma,
            dma, dma((NZ,)), dma, dma,
            dma, dma((OWN,)),
        ],
        compiler_params=pltpu.CompilerParams(has_side_effects=True, vmem_limit_bytes=56 * 1024 * 1024),
    )(queries, key_rows, value_rows, step_rates, own)


def solution(mesh):
    torus = Mesh(mesh.devices.reshape(NZ, 2, NX, 4, 2), AXES)
    seq = ("z", "yl", "x")
    head = ("yh", "c")
    return jax.shard_map(
        shards,
        mesh=torus,
        in_specs=(
            P((*seq, *head), None),
            P((*seq, *head), None),
            P((*seq, *head), None),
            P((*seq, *head), None),
            P(seq, head, None),
            P(seq, head, None),
            P(seq, head, None),
        ),
        out_specs=P((*seq, *head), None),
        check_vma=False,
    )
```

time: 373 us -> 146 us (0.39)
  the two profiles are of different devices: /device:TPU:64 before, /device:TPU:1 now
where the time goes in v1:
time: 146 us
  Pallas kernels  141 us (97%)
  local copies, waits for them, and re-layouts  3.09 us (2%)
    pallas_call x1, Pallas kernels, shards(): pl.pallas_call(fast_kernel, out_shape=jax.ShapeDtypeStruct((ROWS, D), BF1...  141 us
    unnamed x4, local copies, waits for them, and re-layouts  3.09 us

profile of v1, /device:TPU:1, one launch (start us, length us, event | category | flops | bytes accessed | tf_op | source)
XLA Modules:
  0.0 145.6 jit_solution(4183041315896109041)
XLA Ops:
  0.0 0.7 maximum_bitcast_fusion
  0.7 0.0 copy-start
  0.7 0.6 pad_maximum_fusion.w_ref
  1.4 0.1 copy-done
  1.4 0.7 copy.8.rate_ref
  2.2 141.1 %shard_map.73 = bf16[128,4096]{1,0:T(8,128)(2,1)} custom-call(bf16[128,4096]{1,0:T(8,128)(2,1)} %q_hbm.1, bf16[128,4096]{1,0:T(8,128)(2,1)} %k_hbm.1, bf16[128,4096]{1,0:T(8,128)(2,1)} %v_hbm.1, bf16[128,8]{1,0:T(8,128)(2,1)} %copy.8.rate_ref, bf16[16,768]{1,0:T(8,128)(2,1)} %pad_maximum_fusion.w_ref), custom_call_target="tpu_custom_call" | custom-call | tf_op jit(solution)/shard_map/pallas_call | solution.py:358
  143.3 2.3 %copy.10 = bf16[128,4096]{1,0:T(8,128)(2,1)} copy(bf16[128,4096]{1,0:T(8,128)(2,1)} %shard_map.73) | data formatting | bytes 2097152
  (1 shorter events, 0.0 us)
Async XLA Ops:
  0.7 0.7 copy-start

commit v2 on v1

--- a/solution.py
+++ b/solution.py
@@ -25,17 +25,20 @@
 
 
 def fast_kernel(
-    q_hbm, k_hbm, v_hbm, rate_ref, w_ref, out_ref,
-    ql, kl, vl, tl, halo, kb, vb, qb, wrecv, wfull, gu, hid, gown, gsend, gex, gb, rsb, agb, wnew, fo, ret, att,
-    lsem, wsend, wrecv_sem, wfsend, wfrecv, ksend, krecv, vsend, vrecv, qsend, qrecv, hsend, hrecv,
-    exsend, exrecv, rssend, rsrecv, agsend, agrecv, agfsend, agfrecv, osend, orecv,
+    q_hbm, k_hbm, v_hbm, rate_ref, wg_ref, wu_ref, wd_ref, out_ref,
+    ql, kl, vl, tl, halo, kb, vb, qb, wpack, wrecv, wfull, gu, hid, gown, gsend, gex, gb, near, part_sum, far, agb, wnew, fo, ret, att,
+    lsem, wcsend, wcrecv, wtsend, wtrecv, wssend, wsrecv, wfsend, wfrecv, ksend, krecv, vsend, vrecv, qsend, qrecv,
+    hsend, hrecv, exsend, exrecv, nsend, nrecv, fsend, frecv, atsend, atrecv, assend, asrecv, afsend, afrecv, osend, orecv,
 ):
     z, yl, x, yh, c = (lax.axis_index(a) for a in AXES)
     y = 2 * yh + yl
     colour = lax.rem(2 * x + y + 3 * z, 8)
     sign = 1 - 2 * c
     other = (z, yl, x, yh, 1 - c)
-    spot = z * NX + x
+    skew = 2 * (1 - c)
+    line = lax.rem(z - skew * x + 64, NZ)
+    spot = line * NX + x
+    place = (((z * 2 + yl) * NX + x) * 4 + yh) * 2 + c
 
     def device(px, py, pz, core):
         py = lax.rem(py + 64, NY)
@@ -57,38 +60,113 @@
     def columns(head):
         return pl.ds(pl.multiple_of(head * HS, HS), HS)
 
+    def near_mate(step):
+        dz = skew * step
+        return device(x + step, y - 2 * step - 3 * dz, z + dz, c)
+
+    def far_mate(step):
+        return device(x, y - 3 * step, z + step, c)
+
+    def block_at(index):
+        index = lax.rem(index + 512, 512)
+        return (index // 64, lax.rem(index // 32, 2), lax.rem(index // 8, 4), lax.rem(index // 2, 4), lax.rem(index, 2))
+
+    my_head = 2 * yh + c
+    is_self = (my_head == colour) & (yl == c)
+    weight_dest = device(x, my_head - 2 * x - 3 * z, z, yl)
+    weight_source = (z, c, x, colour // 2, lax.rem(colour, 2))
+
+    barrier = pltpu.get_barrier_semaphore()
+    partners = [there(way) for way in range(OWN)] + [there(OWN - 1, -1), other, block_at(place + 1), block_at(place - 1)]
+    partners += [near_mate(step) for step in range(1, NX)] + [far_mate(step) for step in range(1, NZ)]
+
+    def greet(dev):
+        pl.semaphore_signal(barrier, inc=1, device_id=dev, device_id_type=MESH)
+
+    for dev in partners:
+        greet(dev)
+
+    @pl.when(jnp.logical_not(is_self))
+    def _():
+        greet(weight_dest)
+        greet(weight_source)
+
     loads = [pltpu.make_async_copy(v_hbm, vl, lsem.at[0]), pltpu.make_async_copy(k_hbm, kl, lsem.at[1]),
              pltpu.make_async_copy(q_hbm, ql, lsem.at[2])]
     for load in loads:
         load.start()
+    gate_rows, up_rows, down_rows = (ref[...].astype(F32) for ref in (wg_ref, wu_ref, wd_ref))
+    wpack[...] = jnp.concatenate(
+        [jnp.concatenate([gate_rows, up_rows[:, : HS // 2]], 1), jnp.concatenate([up_rows[:, HS // 2 :], down_rows], 1)], 0
+    ).astype(BF16)
+
+    @pl.when(is_self)
+    def _():
+        pl.semaphore_wait(barrier, len(partners))
+
+    @pl.when(jnp.logical_not(is_self))
+    def _():
+        pl.semaphore_wait(barrier, len(partners) + 2)
+
+    dest_spot = lax.rem(z - 2 * (1 - yl) * x + 64, NZ) * NX + x
+
+    @pl.when(is_self)
+    def _():
+        wrecv[yl, dest_spot] = wpack[...]
+
+    @pl.when(jnp.logical_not(is_self))
+    def _():
+        remote(wpack, wrecv.at[yl, dest_spot], wcsend, wcrecv, weight_dest).start()
+
     for way in range(OWN):
         remote(k_hbm.at[:, columns(head_of(way))], kb.at[way], ksend, krecv.at[way], there(way)).start()
 
-    my_head = 2 * yh + c
-    is_self = (my_head == colour) & (yl == c)
-
-    def weight_dest(dx, dz):
-        px, pz = x + dx, z + dz
-        return device(px, my_head - 2 * px - 3 * pz, pz, yl)
-
-    @pl.when(is_self)
-    def _():
-        wrecv[yl, spot] = w_ref[...]
+    def far_sends(buffer, send, recv):
+        def go(step, carry):
+            block = buffer.at[c, spot]
+            remote(block, block, send, recv.at[step], far_mate(step)).start()
+            return carry
+
+        lax.fori_loop(1, NZ, go, 0)
+
+    def near_sends(buffer, send, recv, nsend_, nrecv_):
+        def go(step, carry):
+            block = buffer.at[c, lax.rem(line - step + NZ, NZ) * NX + x]
+
+            @pl.when(step > 0)
+            def _():
+                remote(block, block, send, recv.at[step], other).wait_recv()
+
+            for move in range(1, NX):
+                remote(block, block, nsend_, nrecv_.at[step], near_mate(move)).start()
+            return carry
+
+        lax.fori_loop(0, NZ, go, 0)
+
+    def cross_sends(buffer, nsend_, nrecv_, csend, crecv, beside=None):
+        def go(step, carry):
+            if beside is not None:
+                beside(step, 0)
+            three = buffer.at[c, pl.ds(0, NX - 1)]
+            remote(three, three, nsend_, nrecv_.at[step], other).wait_recv()
+            four = buffer.at[c, pl.ds(lax.rem(line - step + NZ, NZ) * NX, NX)]
+            remote(four, four, csend, crecv, other).start()
+            return carry
+
+        lax.fori_loop(0, NZ, go, 0)
+
+    def crossed(buffer, csend, crecv):
+        remote(buffer.at[1 - c], buffer.at[1 - c], csend, crecv, other).wait_recv()
 
     @pl.when(jnp.logical_not(is_self))
     def _():
-        remote(w_ref, wrecv.at[yl, spot], wsend, wrecv_sem.at[0], weight_dest(0, 0)).start()
-
-    def send_weights(i, carry):
-        dx, dz = lax.rem(i, NX), i // NX
-        remote(w_ref, wrecv.at[yl, spot], wsend, wrecv_sem.at[dz], weight_dest(dx, dz)).start()
-        return carry
-
-    lax.fori_loop(1, NX * NZ, send_weights, 0)
-
+        remote(wpack, wpack, wcsend, wcrecv, other).wait_recv()
+
+    far_sends(wrecv, wtsend, wtrecv)
+    rates = jnp.transpose(rate_ref[...].astype(F32))
     loads[0].wait()
     for head in range(HEADS):
-        rate = rate_ref[:, head : head + 1].astype(F32)
+        rate = rates[:, head : head + 1]
         tl[head] = (-rate * vl[:, head * HS : (head + 1) * HS].astype(F32)).astype(BF16)
     for way in range(OWN):
         remote(tl.at[head_of(way)], vb.at[way], vsend, vrecv.at[way], there(way)).start()
@@ -96,33 +174,20 @@
     loads[1].wait()
     kb[OWN] = kl[:, columns(colour)]
 
-    def unpack(half, pz):
-        for pair in range(NX // 2):
-            one = wrecv[half, pz * NX + 2 * pair].astype(F32)
-            two = wrecv[half, pz * NX + 2 * pair + 1].astype(F32)
-            rows = pl.ds(pl.multiple_of(((pz * 2 + half) * NX + 2 * pair) * 8, 16), 16)
-            wfull[rows, : 3 * HS // 2] = jnp.concatenate([one[:8], two[:8]], 0).astype(BF16)
-            wfull[rows, 3 * HS // 2 :] = jnp.concatenate([one[8:], two[8:]], 0).astype(BF16)
-
-    def weights_in(dz, carry):
-        pz = lax.rem(z - dz + NZ, NZ)
-
-        @pl.when(is_self & (dz == 0))
-        def _():
-            part = wrecv.at[c, pl.ds(0, NX - 1)]
-            remote(part, part, wsend, wrecv_sem.at[dz], other).wait_recv()
-
-        @pl.when(jnp.logical_not(is_self & (dz == 0)))
-        def _():
-            part = wrecv.at[c, pl.ds(0, NX)]
-            remote(part, part, wsend, wrecv_sem.at[dz], other).wait_recv()
-
-        part = wrecv.at[c, pl.ds(pz * NX, NX)]
-        remote(part, part, wfsend, wfrecv, other).start()
-        unpack(c, pz)
-        return carry
-
-    lax.fori_loop(0, NZ, weights_in, 0)
+    near_sends(wrecv, wtsend, wtrecv, wssend, wsrecv)
+
+    def unpack(half):
+        def rows_of(pz, carry):
+            for px in range(0, NX, 2):
+                one, two = (
+                    wrecv[half, lax.rem(pz - 2 * (1 - half) * at + 64, NZ) * NX + at].astype(F32) for at in (px, px + 1)
+                )
+                rows = pl.ds(pl.multiple_of(((pz * 2 + half) * NX + px) * 8, 16), 16)
+                wfull[rows, : 3 * HS // 2] = jnp.concatenate([one[:8], two[:8]], 0).astype(BF16)
+                wfull[rows, 3 * HS // 2 :] = jnp.concatenate([one[8:], two[8:]], 0).astype(BF16)
+            return carry
+
+        lax.fori_loop(0, NZ, rows_of, 0)
 
     def normed(block):
         wide = block.astype(F32)
@@ -133,22 +198,17 @@
             remote(kb.at[way], kb.at[way], ksend, krecv.at[way], other).wait_recv()
         kb[way] = normed(kb[way])
 
-    remote(wrecv.at[1 - c], wrecv.at[1 - c], wfsend, wfrecv, other).wait_recv()
-
-    def unpack_other(pz, carry):
-        unpack(1 - c, pz)
-        return carry
-
-    lax.fori_loop(0, NZ, unpack_other, 0)
+    cross_sends(wrecv, wssend, wsrecv, wfsend, wfrecv)
+    unpack(c)
+    crossed(wrecv, wfsend, wfrecv)
+    unpack(1 - c)
 
     for way in range(OWN):
         remote(vb.at[way], vb.at[way], vsend, vrecv.at[way], other).wait_recv()
 
     for way in range(OWN):
         remote(q_hbm.at[:, columns(head_of(way))], qb.at[way], qsend, qrecv.at[way], there(way)).start()
-    place = (((z * 2 + yl) * NX + x) * 4 + yh) * 2 + c
-    after = lax.rem(place + 1, 512)
-    next_block = (after // 64, lax.rem(after // 32, 2), lax.rem(after // 8, 4), lax.rem(after // 2, 4), lax.rem(after, 2))
+    next_block = block_at(place + 1)
     remote(kl.at[pl.ds(ROWS - WINDOW, WINDOW)], halo.at[0], hsend, hrecv, next_block).start()
     remote(vl.at[pl.ds(ROWS - WINDOW, WINDOW)], halo.at[1], hsend, hrecv, next_block).start()
     loads[2].wait()
@@ -195,29 +255,39 @@
     half_sums(c, gown)
     exchange.wait_recv()
 
-    def mate(dx, dz):
-        return device(x + dx, y - 2 * dx - 3 * dz, z + dz, c)
-
-    def send_sums(dz, carry):
-        pz = lax.rem(z + dz, NZ)
-        rows = pl.ds(pl.multiple_of(pz * 64, 64), 64)
-        gb[pl.ds(pz * NX, NX)] = (gown[rows, :] + gex[rows, :].astype(F32)).astype(BF16).reshape(NX, 16, 3 * HS // 2)
-        for dx in range(NX):
-            px = lax.rem(x + dx, NX)
-
-            def go():
-                remote(gb.at[pz * NX + px], rsb.at[spot], rssend, rsrecv, mate(dx, dz)).start()
-
-            if dx == 0:
-                pl.when(dz > 0)(go)
-            else:
-                go()
+    def near_sums(i, carry):
+        step = lax.rem(i + 1, NZ)
+        to = lax.rem(line + step, NZ)
+        rows = pl.ds(pl.multiple_of(to * 64, 64), 64)
+        gb[pl.ds(to * NX, NX)] = (gown[rows, :] + gex[rows, :].astype(F32)).astype(BF16).reshape(NX, 16, 3 * HS // 2)
+        for move in range(1, NX):
+            block = gb.at[to * NX + lax.rem(x + move, NX)]
+            remote(block, near.at[to * NX + x], nsend, nrecv.at[step], near_mate(move)).start()
         return carry
 
-    lax.fori_loop(0, NZ, send_sums, 0)
-    rsb[spot] = gb[spot]
-
-    remote(halo, halo, hsend, hrecv, other).wait_recv()
+    lax.fori_loop(0, NZ, near_sums, 0)
+
+    for way in range(OWN):
+        remote(qb.at[way], qb.at[way], qsend, qrecv.at[way], other).wait_recv()
+        qb[way] = normed(qb[way])
+
+    def far_sums(i, carry):
+        step = lax.rem(i + 1, NZ)
+        to = lax.rem(line + step, NZ)
+        three = near.at[pl.ds(0, NX - 1)]
+        remote(three, three, nsend, nrecv.at[step], other).wait_recv()
+        near[to * NX + x] = gb[to * NX + x]
+        part_sum[to] = jnp.sum(near[pl.ds(to * NX, NX)].astype(F32), axis=0).astype(BF16)
+
+        @pl.when(step > 0)
+        def _():
+            remote(part_sum.at[to], far.at[line], fsend, frecv, far_mate(step)).start()
+
+        return carry
+
+    lax.fori_loop(0, NZ, far_sums, 0)
+    far[line] = part_sum[line]
+
     span_rows = ROWS + WINDOW
     at_row = lax.broadcasted_iota(jnp.int32, (ROWS, span_rows), 0)
     at_key = lax.broadcasted_iota(jnp.int32, (ROWS, span_rows), 1)
@@ -241,46 +311,14 @@
             att[head, :, part] = mixed / totals
         return carry
 
-    lax.fori_loop(0, HEADS, attend, 0)
-
-    for way in range(OWN):
-        remote(qb.at[way], qb.at[way], qsend, qrecv.at[way], other).wait_recv()
-        qb[way] = normed(qb[way])
-
-    others = rsb.at[pl.ds(0, NX * NZ - 1)]
-    remote(others, others, rssend, rsrecv, other).wait_recv()
-
-    def add_up(i, total):
-        return total + jnp.sum(rsb[pl.ds(i * NX, NX)].astype(F32), axis=0)
-
-    agb[c, spot] = lax.fori_loop(0, NZ, add_up, jnp.zeros((16, 3 * HS // 2), F32)).astype(BF16)
-
-    def spread(i, carry):
-        dx, dz = lax.rem(i, NX), i // NX
-        remote(agb.at[c, spot], agb.at[c, spot], agsend, agrecv.at[dz], mate(dx, dz)).start()
-        return carry
-
-    lax.fori_loop(1, NX * NZ, spread, 0)
-
-    def sums_in(dz, carry):
-        pz = lax.rem(z - dz + NZ, NZ)
-
-        @pl.when(dz == 0)
-        def _():
-            part = agb.at[c, pl.ds(0, NX - 1)]
-            remote(part, part, agsend, agrecv.at[dz], other).wait_recv()
-
-        @pl.when(dz > 0)
-        def _():
-            part = agb.at[c, pl.ds(0, NX)]
-            remote(part, part, agsend, agrecv.at[dz], other).wait_recv()
-
-        part = agb.at[c, pl.ds(pz * NX, NX)]
-        remote(part, part, agfsend, agfrecv, other).start()
-        return carry
-
-    lax.fori_loop(0, NZ, sums_in, 0)
-    remote(agb.at[1 - c], agb.at[1 - c], agfsend, agfrecv, other).wait_recv()
+    seven = far.at[pl.ds(0, NZ - 1)]
+    remote(seven, seven, fsend, frecv, other).wait_recv()
+    agb[c, spot] = jnp.sum(far[...].astype(F32), axis=0).astype(BF16)
+    far_sends(agb, atsend, atrecv)
+    near_sends(agb, atsend, atrecv, assend, asrecv)
+    remote(halo, halo, hsend, hrecv, other).wait_recv()
+    cross_sends(agb, assend, asrecv, afsend, afrecv, attend)
+    crossed(agb, afsend, afrecv)
 
     def squares(i, total):
         for half in range(2):
@@ -330,26 +368,21 @@
         remote(sent, sent, sem, orecv.at[0], other).wait_send()
     remote(halo, halo, hsend, hrecv, other).wait_send()
     exchange.wait_send()
-    for buffer, sem in ((rsb, rssend), (agb.at[0], agsend)):
-        sent = buffer.at[pl.ds(0, NX * NZ - 1)]
+    for buffer, sem in ((near, nsend), (wrecv.at[0], wssend), (agb.at[0], assend)):
+        sent = buffer.at[pl.ds(0, NZ * (NX - 1))]
         remote(sent, sent, sem, orecv.at[0], other).wait_send()
-
-    @pl.when(is_self)
-    def _():
-        sent = wrecv.at[0, pl.ds(0, NX * NZ - 1)]
-        remote(sent, sent, wsend, orecv.at[0], other).wait_send()
+    for sem in (fsend, wtsend, atsend):
+        remote(seven, seven, sem, orecv.at[0], other).wait_send()
 
     @pl.when(jnp.logical_not(is_self))
     def _():
-        remote(wrecv.at[0], wrecv.at[0], wsend, orecv.at[0], other).wait_send()
-
-    for buffer, sem in ((wrecv.at[0], wfsend), (agb.at[0], agfsend)):
+        remote(wpack, wpack, wcsend, orecv.at[0], other).wait_send()
+
+    for buffer, sem in ((wrecv.at[0], wfsend), (agb.at[0], afsend)):
         remote(buffer, buffer, sem, orecv.at[0], other).wait_send()
 
 
 def shards(queries, key_rows, value_rows, step_rates, w_gate, w_up, w_down):
-    own = jnp.concatenate([w_gate, w_up, w_down], 2).reshape(8, 3 * HS)
-    own = jnp.concatenate([own[:, : 3 * HS // 2], own[:, 3 * HS // 2 :]], 0)
     hbm = pl.BlockSpec(memory_space=pl.ANY)
     vmem = pl.BlockSpec(memory_space=pltpu.VMEM)
     wide = 3 * HS // 2
@@ -358,7 +391,7 @@
     return pl.pallas_call(
         fast_kernel,
         out_shape=jax.ShapeDtypeStruct((ROWS, D), BF16),
-        in_specs=[hbm, hbm, hbm, vmem, vmem],
+        in_specs=[hbm, hbm, hbm, vmem, vmem, vmem, vmem],
         out_specs=vmem,
         scratch_shapes=[
             pltpu.VMEM((ROWS, D), BF16),
@@ -369,6 +402,7 @@
             blocks,
             blocks,
             blocks,
+            pltpu.VMEM((16, wide), BF16),
             pltpu.VMEM((2, NZ * NX, 16, wide), BF16),
             pltpu.VMEM((HS, 3 * HS), BF16),
             pltpu.VMEM((2, 8, ROWS, HS), BF16),
@@ -378,22 +412,24 @@
             pltpu.VMEM((HS, wide), BF16),
             pltpu.VMEM((NZ * NX, 16, wide), BF16),
             pltpu.VMEM((NZ * NX, 16, wide), BF16),
+            pltpu.VMEM((NZ, 16, wide), BF16),
+            pltpu.VMEM((NZ, 16, wide), BF16),
             pltpu.VMEM((2, NZ * NX, 16, wide), BF16),
             pltpu.VMEM((HS, 3 * HS), BF16),
             blocks,
             blocks,
             pltpu.VMEM((8, ROWS, HS), F32),
             dma((3,)),
-            dma, dma((NZ,)), dma, dma,
+            dma, dma, dma, dma((NZ,)), dma, dma((NZ,)), dma, dma,
             dma, dma((OWN,)), dma, dma((OWN,)), dma, dma((OWN,)),
             dma, dma,
             dma, dma,
-            dma, dma,
             dma, dma((NZ,)), dma, dma,
+            dma, dma((NZ,)), dma, dma((NZ,)), dma, dma,
             dma, dma((OWN,)),
         ],
-        compiler_params=pltpu.CompilerParams(has_side_effects=True, vmem_limit_bytes=56 * 1024 * 1024),
-    )(queries, key_rows, value_rows, step_rates, own)
+        compiler_params=pltpu.CompilerParams(collective_id=0, has_side_effects=True, vmem_limit_bytes=56 * 1024 * 1024),
+    )(queries, key_rows, value_rows, jnp.transpose(step_rates), *(w.reshape(8, HS) for w in (w_gate, w_up, w_down)))
 
 
 def solution(mesh):

time: 146 us -> 127 us (0.87)
  Pallas kernels: 141 us -> 124 us
    pallas_call x1, Pallas kernels: 141 us -> 124 us  [shards(): pl.pallas_call(fast_kernel, out_shape=jax.ShapeDtypeStruct((ROWS, D), BF1...]
    unnamed x4 -> x1, local copies, waits for them, and re-layouts: 3.09 us -> 2.29 us
where the time goes in v2:
time: 127 us; the launch traced here: 126 us
  Pallas kernels  124 us (98%)
  local copies, waits for them, and re-layouts  2.29 us (2%)
    pallas_call x1, Pallas kernels, shards(): pl.pallas_call(fast_kernel, out_shape=jax.ShapeDtypeStruct((ROWS, D), BF1...  124 us

profile of v2, /device:TPU:1, one launch (start us, length us, event | category | flops | bytes accessed | tf_op | source)
XLA Modules:
  0.0 126.4 jit_solution(1358706141316809011)
XLA Ops:
  0.0 124.1 %shard_map.73 = bf16[128,4096]{1,0:T(8,128)(2,1)} custom-call(bf16[128,4096]{1,0:T(8,128)(2,1)} %q_hbm.1, bf16[128,4096]{1,0:T(8,128)(2,1)} %k_hbm.1, bf16[128,4096]{1,0:T(8,128)(2,1)} %v_hbm.1, bf16[8,128]{1,0:T(8,128)(2,1)} %bitcast.7, bf16[8,512]{1,0:T(8,128)(2,1)} %bitcast.4, bf16[8,512]{1,0:T(8,128)(2,1)} %bitcast.5, bf16[8,512]{1,0:T(8,128)(2,1)} %bitcast.6), custom_call_target="tpu_custom_call" | custom-call | tf_op jit(solution)/shard_map/pallas_call | solution.py:391
  124.1 2.3 %copy.9 = bf16[128,4096]{1,0:T(8,128)(2,1)} copy(bf16[128,4096]{1,0:T(8,128)(2,1)} %shard_map.73) | data formatting | bytes 2097152

commit v3 on v2

--- a/solution.py
+++ b/solution.py
@@ -26,9 +26,9 @@
 
 def fast_kernel(
     q_hbm, k_hbm, v_hbm, rate_ref, wg_ref, wu_ref, wd_ref, out_ref,
-    ql, kl, vl, tl, halo, kb, vb, qb, wpack, wrecv, wfull, gu, hid, gown, gsend, gex, gb, near, part_sum, far, agb, wnew, fo, ret, att,
+    ql, kl, vl, tl, edge_q, edge_o, edge_in, stat_o, stat_in, stat_own, kb, vb, qb, wpack, wrecv, wfull, gu, hid, gown, gsend, gex, gb, near, part_sum, far, agb, wnew, fo, ret, att,
     lsem, wcsend, wcrecv, wtsend, wtrecv, wssend, wsrecv, wfsend, wfrecv, ksend, krecv, vsend, vrecv, qsend, qrecv,
-    hsend, hrecv, exsend, exrecv, nsend, nrecv, fsend, frecv, atsend, atrecv, assend, asrecv, afsend, afrecv, osend, orecv,
+    hqsend, hqrecv, hosend, horecv, hssend, hsrecv, exsend, exrecv, nsend, nrecv, fsend, frecv, atsend, atrecv, assend, asrecv, afsend, afrecv, osend, orecv,
 ):
     z, yl, x, yh, c = (lax.axis_index(a) for a in AXES)
     y = 2 * yh + yl
@@ -208,9 +208,8 @@
 
     for way in range(OWN):
         remote(q_hbm.at[:, columns(head_of(way))], qb.at[way], qsend, qrecv.at[way], there(way)).start()
-    next_block = block_at(place + 1)
-    remote(kl.at[pl.ds(ROWS - WINDOW, WINDOW)], halo.at[0], hsend, hrecv, next_block).start()
-    remote(vl.at[pl.ds(ROWS - WINDOW, WINDOW)], halo.at[1], hsend, hrecv, next_block).start()
+    edge = q_hbm.at[pl.ds(0, WINDOW)]
+    remote(edge, edge_q, hqsend, hqrecv, block_at(place - 1)).start()
     loads[2].wait()
     qb[OWN] = normed(ql[:, columns(colour)])
 
@@ -255,6 +254,72 @@
     half_sums(c, gown)
     exchange.wait_recv()
 
+    scale = 1.0 / math.sqrt(HEAD_DIM)
+    by_column = (((1,), (1,)), ((), ()))
+    edge_row = lax.broadcasted_iota(jnp.int32, (WINDOW, WINDOW), 0)
+    edge_key = lax.broadcasted_iota(jnp.int32, (WINDOW, WINDOW), 1)
+    in_window = edge_key > edge_row
+    stat_lane = lax.broadcasted_iota(jnp.int32, (WINDOW, HEAD_DIM), 1)
+    next_block = block_at(place + 1)
+    stat_o[...] = jnp.zeros_like(stat_o)
+
+    def attend_edge(head, carry):
+        cols = columns(head)
+        queries = edge_q[:, cols]
+        keys, values = (ref[pl.ds(ROWS - WINDOW, WINDOW), cols] for ref in (kl, vl))
+        stats = stat_o[...]
+        for sub in range(HS // HEAD_DIM):
+            part = slice(sub * HEAD_DIM, (sub + 1) * HEAD_DIM)
+            scores = lax.dot_general(queries[:, part], keys[:, part], by_column, preferred_element_type=F32) * scale
+            masked = jnp.where(in_window, scores, -1e30)
+            maximum = jnp.max(masked, axis=1, keepdims=True)
+            weights = jnp.where(in_window, jnp.exp(masked - maximum), 0.0)
+            totals = jnp.sum(weights, axis=1, keepdims=True)
+            edge_o[head, :, part] = jnp.dot(weights.astype(BF16), values[:, part], preferred_element_type=F32).astype(BF16)
+            lane = head * (HS // HEAD_DIM) + sub
+            stats = jnp.where(stat_lane == lane, maximum, jnp.where(stat_lane == lane + 32, totals, stats))
+        stat_o[...] = stats
+        return carry
+
+    at_row = lax.broadcasted_iota(jnp.int32, (ROWS, ROWS), 0)
+    at_key = lax.broadcasted_iota(jnp.int32, (ROWS, ROWS), 1)
+    allowed = (at_key > at_row - WINDOW) & (at_key <= at_row)
+
+    def attend(head):
+        cols = columns(head)
+        queries, keys, values = ql[:, cols], kl[:, cols], vl[:, cols]
+        stats = jnp.zeros((WINDOW, HEAD_DIM), F32)
+        for sub in range(HS // HEAD_DIM):
+            part = slice(sub * HEAD_DIM, (sub + 1) * HEAD_DIM)
+            scores = lax.dot_general(queries[:, part], keys[:, part], by_column, preferred_element_type=F32) * scale
+            masked = jnp.where(allowed, scores, -1e30)
+            maximum = jnp.max(masked, axis=1, keepdims=True)
+            weights = jnp.where(allowed, jnp.exp(masked - maximum), 0.0)
+            totals = jnp.sum(weights, axis=1, keepdims=True)
+            mixed = jnp.dot(weights.astype(BF16), values[:, part], preferred_element_type=F32)
+            stats = jnp.where(
+                stat_lane == sub, maximum[:WINDOW], jnp.where(stat_lane == sub + 4, totals[:WINDOW], stats)
+            )
+            att[head, :WINDOW, part] = mixed[:WINDOW]
+            att[head, WINDOW:, part] = mixed[WINDOW:] / totals[WINDOW:]
+        stat_own[head] = stats
+
+    def merge(head, carry):
+        stats, own = stat_in[...], stat_own[head]
+        for sub in range(HS // HEAD_DIM):
+            part = slice(sub * HEAD_DIM, (sub + 1) * HEAD_DIM)
+            lane = head * (HS // HEAD_DIM) + sub
+            edge_max, edge_total = (
+                jnp.sum(jnp.where(stat_lane == at, stats, 0.0), axis=1, keepdims=True) for at in (lane, lane + 32)
+            )
+            edge_max = jnp.where(place == 0, -1e30, edge_max)
+            maximum, totals = own[:, sub : sub + 1], own[:, sub + 4 : sub + 5]
+            both_max = jnp.maximum(maximum, edge_max)
+            here, before = jnp.exp(maximum - both_max), jnp.exp(edge_max - both_max)
+            first = att[head, :WINDOW, part] * here + edge_in[head, :, part].astype(F32) * before
+            att[head, :WINDOW, part] = first / (totals * here + edge_total * before)
+        return carry
+
     def near_sums(i, carry):
         step = lax.rem(i + 1, NZ)
         to = lax.rem(line + step, NZ)
@@ -272,6 +337,7 @@
         qb[way] = normed(qb[way])
 
     def far_sums(i, carry):
+        attend(i)
         step = lax.rem(i + 1, NZ)
         to = lax.rem(line + step, NZ)
         three = near.at[pl.ds(0, NX - 1)]
@@ -288,36 +354,15 @@
     lax.fori_loop(0, NZ, far_sums, 0)
     far[line] = part_sum[line]
 
-    span_rows = ROWS + WINDOW
-    at_row = lax.broadcasted_iota(jnp.int32, (ROWS, span_rows), 0)
-    at_key = lax.broadcasted_iota(jnp.int32, (ROWS, span_rows), 1)
-    allowed = (at_key > at_row) & (at_key <= at_row + WINDOW) & (at_key + place * ROWS >= WINDOW)
-
-    def attend(head, carry):
-        cols = columns(head)
-        queries = ql[:, cols]
-        keys = jnp.concatenate([halo[0, :, cols], kl[:, cols]], 0)
-        values = jnp.concatenate([halo[1, :, cols], vl[:, cols]], 0)
-        for sub in range(HS // HEAD_DIM):
-            part = slice(sub * HEAD_DIM, (sub + 1) * HEAD_DIM)
-            scores = lax.dot_general(
-                queries[:, part], keys[:, part], (((1,), (1,)), ((), ())), preferred_element_type=F32
-            ) * (1.0 / math.sqrt(HEAD_DIM))
-            masked = jnp.where(allowed, scores, -1e30)
-            maximum = jnp.max(masked, axis=1, keepdims=True)
-            weights = jnp.where(allowed, jnp.exp(masked - maximum), 0.0)
-            totals = jnp.sum(weights, axis=1, keepdims=True)
-            mixed = jnp.dot(weights.astype(BF16), values[:, part], preferred_element_type=F32)
-            att[head, :, part] = mixed / totals
-        return carry
-
     seven = far.at[pl.ds(0, NZ - 1)]
     remote(seven, seven, fsend, frecv, other).wait_recv()
     agb[c, spot] = jnp.sum(far[...].astype(F32), axis=0).astype(BF16)
     far_sends(agb, atsend, atrecv)
     near_sends(agb, atsend, atrecv, assend, asrecv)
-    remote(halo, halo, hsend, hrecv, other).wait_recv()
-    cross_sends(agb, assend, asrecv, afsend, afrecv, attend)
+    remote(edge_q, edge_q, hqsend, hqrecv, other).wait_recv()
+    cross_sends(agb, assend, asrecv, afsend, afrecv, attend_edge)
+    remote(edge_o, edge_in, hosend, horecv, next_block).start()
+    remote(stat_o, stat_in, hssend, hsrecv, next_block).start()
     crossed(agb, afsend, afrecv)
 
     def squares(i, total):
@@ -356,6 +401,9 @@
         for way in (2 * pair, 2 * pair + 1):
             if way < OWN:
                 remote(fo.at[way], ret.at[way], osend, orecv.at[way], there(way, -1)).start()
+    remote(edge_in, edge_in, hosend, horecv, other).wait_recv()
+    remote(stat_in, stat_in, hssend, hsrecv, other).wait_recv()
+    lax.fori_loop(0, HEADS, merge, 0)
     ret[OWN] = fo[OWN]
     for way in (OWN, *range(OWN)):
         if way < OWN:
@@ -366,7 +414,8 @@
     for buffer, sem in ((kb, ksend), (vb, vsend), (qb, qsend), (ret, osend)):
         sent = buffer.at[pl.ds(0, OWN)]
         remote(sent, sent, sem, orecv.at[0], other).wait_send()
-    remote(halo, halo, hsend, hrecv, other).wait_send()
+    for buffer, sem in ((edge_q, hqsend), (edge_in, hosend), (stat_in, hssend)):
+        remote(buffer, buffer, sem, orecv.at[0], other).wait_send()
     exchange.wait_send()
     for buffer, sem in ((near, nsend), (wrecv.at[0], wssend), (agb.at[0], assend)):
         sent = buffer.at[pl.ds(0, NZ * (NX - 1))]
@@ -398,7 +447,12 @@
             pltpu.VMEM((ROWS, D), BF16),
             pltpu.VMEM((ROWS, D), BF16),
             blocks,
-            pltpu.VMEM((2, WINDOW, D), BF16),
+            pltpu.VMEM((WINDOW, D), BF16),
+            pltpu.VMEM((8, WINDOW, HS), BF16),
+            pltpu.VMEM((8, WINDOW, HS), BF16),
+            pltpu.VMEM((WINDOW, HEAD_DIM), F32),
+            pltpu.VMEM((WINDOW, HEAD_DIM), F32),
+            pltpu.VMEM((8, WINDOW, HEAD_DIM), F32),
             blocks,
             blocks,
             blocks,
@@ -422,7 +476,7 @@
             dma((3,)),
             dma, dma, dma, dma((NZ,)), dma, dma((NZ,)), dma, dma,
             dma, dma((OWN,)), dma, dma((OWN,)), dma, dma((OWN,)),
-            dma, dma,
+            dma, dma, dma, dma, dma, dma,
             dma, dma,
             dma, dma((NZ,)), dma, dma,
             dma, dma((NZ,)), dma, dma((NZ,)), dma, dma,

time: 127 us -> 122 us (0.961)
  the two profiles are of different devices: /device:TPU:1 before, /device:TPU:64 now
where the time goes in v3:
time: 122 us
  Pallas kernels  120 us (98%)
  local copies, waits for them, and re-layouts  2.29 us (2%)
    pallas_call x1, Pallas kernels, shards(): pl.pallas_call(fast_kernel, out_shape=jax.ShapeDtypeStruct((ROWS, D), BF1...  120 us

profile of v3, /device:TPU:64, one launch (start us, length us, event | category | flops | bytes accessed | tf_op | source)
XLA Modules:
  0.0 122.2 jit_solution(7284376095443493259)
XLA Ops:
  0.0 119.9 %shard_map.73 = bf16[128,4096]{1,0:T(8,128)(2,1)} custom-call(bf16[128,4096]{1,0:T(8,128)(2,1)} %q_hbm.1, bf16[128,4096]{1,0:T(8,128)(2,1)} %k_hbm.1, bf16[128,4096]{1,0:T(8,128)(2,1)} %v_hbm.1, bf16[8,128]{1,0:T(8,128)(2,1)} %bitcast.7, bf16[8,512]{1,0:T(8,128)(2,1)} %bitcast.4, bf16[8,512]{1,0:T(8,128)(2,1)} %bitcast.5, bf16[8,512]{1,0:T(8,128)(2,1)} %bitcast.6), custom_call_target="tpu_custom_call" | custom-call | tf_op jit(solution)/shard_map/pallas_call | solution.py:440
  119.9 2.3 %copy.9 = bf16[128,4096]{1,0:T(8,128)(2,1)} copy(bf16[128,4096]{1,0:T(8,128)(2,1)} %shard_map.73) | data formatting | bytes 2097152

commit v4 on v3

--- a/solution.py
+++ b/solution.py
@@ -206,8 +206,6 @@
     for way in range(OWN):
         remote(vb.at[way], vb.at[way], vsend, vrecv.at[way], other).wait_recv()
 
-    for way in range(OWN):
-        remote(q_hbm.at[:, columns(head_of(way))], qb.at[way], qsend, qrecv.at[way], there(way)).start()
     edge = q_hbm.at[pl.ds(0, WINDOW)]
     remote(edge, edge_q, hqsend, hqrecv, block_at(place - 1)).start()
     loads[2].wait()
@@ -331,10 +329,8 @@
         return carry
 
     lax.fori_loop(0, NZ, near_sums, 0)
-
     for way in range(OWN):
-        remote(qb.at[way], qb.at[way], qsend, qrecv.at[way], other).wait_recv()
-        qb[way] = normed(qb[way])
+        remote(q_hbm.at[:, columns(head_of(way))], qb.at[way], qsend, qrecv.at[way], there(way)).start()
 
     def far_sums(i, carry):
         attend(i)
@@ -359,6 +355,9 @@
     agb[c, spot] = jnp.sum(far[...].astype(F32), axis=0).astype(BF16)
     far_sends(agb, atsend, atrecv)
     near_sends(agb, atsend, atrecv, assend, asrecv)
+    for way in range(OWN):
+        remote(qb.at[way], qb.at[way], qsend, qrecv.at[way], other).wait_recv()
+        qb[way] = normed(qb[way])
     remote(edge_q, edge_q, hqsend, hqrecv, other).wait_recv()
     cross_sends(agb, assend, asrecv, afsend, afrecv, attend_edge)
     remote(edge_o, edge_in, hosend, horecv, next_block).start()

time: 122 us -> 123 us (level)
  the two profiles are of different devices: /device:TPU:64 before, /device:TPU:4 now
where the time goes in v4:
time: 123 us
  Pallas kernels  121 us (98%)
  local copies, waits for them, and re-layouts  2.29 us (2%)
    pallas_call x1, Pallas kernels, shards(): pl.pallas_call(fast_kernel, out_shape=jax.ShapeDtypeStruct((ROWS, D), BF1...  121 us

profile of v4, /device:TPU:4, one launch (start us, length us, event | category | flops | bytes accessed | tf_op | source)
XLA Modules:
  0.0 123.0 jit_solution(8788770688060992773)
XLA Ops:
  0.0 120.7 %shard_map.73 = bf16[128,4096]{1,0:T(8,128)(2,1)} custom-call(bf16[128,4096]{1,0:T(8,128)(2,1)} %q_hbm.1, bf16[128,4096]{1,0:T(8,128)(2,1)} %k_hbm.1, bf16[128,4096]{1,0:T(8,128)(2,1)} %v_hbm.1, bf16[8,128]{1,0:T(8,128)(2,1)} %bitcast.7, bf16[8,512]{1,0:T(8,128)(2,1)} %bitcast.4, bf16[8,512]{1,0:T(8,128)(2,1)} %bitcast.5, bf16[8,512]{1,0:T(8,128)(2,1)} %bitcast.6), custom_call_target="tpu_custom_call" | custom-call | tf_op jit(solution)/shard_map/pallas_call | solution.py:439
  120.7 2.3 %copy.9 = bf16[128,4096]{1,0:T(8,128)(2,1)} copy(bf16[128,4096]{1,0:T(8,128)(2,1)} %shard_map.73) | data formatting | bytes 2097152
